TPU v7x, 32 devices: a whole 2x2x4 slice. The times are simulated.
32 devices in a mesh: group: 2 (over y), section: 4 (over z), ctx: 2 (over core), head: 2 (over x).
Axes of the slice: x: 2, y: 2, z: 4, core: 2. Of those that a mesh axis runs over, the one named last changes fastest.
Arguments:
- queries: bfloat16 [2048, 48, 128], P(('group', 'section'), 'head'), parts along dimension 0, may hold values from -6 to 6
- slice_kv: bfloat16 [2048, 2, 128], P(('group', 'section')), parts along dimension 0, may hold values from -6 to 6
- cache_keys: bfloat16 [8, 16, 128, 128], P(('group', 'section'), 'ctx'), parts along dimension 0
- cache_values: bfloat16 [8, 16, 128, 128], P(('group', 'section'), 'ctx'), parts along dimension 0, may hold values from -6 to 6
- block_table: int32 [8, 16], P('group'), parts along dimension 0, may hold values from 0 to 15, each once within a row
- slice_index: int32 [8], P('group'), parts along dimension 0, may hold values from 0 to 3, as said below
- out_weight: bfloat16 [48, 128, 6144], P('head', 'section', 'ctx'), may hold values from -0.078125 to 0.078125
Outputs:
- mixed: bfloat16 [2048, 6144], P(('group', 'section'), ('ctx', 'head')), parts along dimension 0
There are 2 independent parts, one for each index of `group`. A program takes and returns all parts, laid end to end along the dimension named above; an argument that names none is the same for every part. Nothing has to cross between parts.
Inputs may be any that keep to these rules, and one draw needn't show every extreme that they name: `slice_index`: every value appears once; the sections s and s + 4 / 2 (for s < 2) hold slice indices that sum to 3.
All inputs are finite; a program needn't handle non-finite values.
Results may differ from a plain program's by a relative error of at most 0.018.
Values may be sent and summed in bfloat16 or wider, within the bound.
A program may use at most 64 MiB of HBM per device.

v0:
```python
import math

import jax
import jax.numpy as jnp
from jax import lax
from jax.sharding import PartitionSpec as P

BPS = 4


negative_floor = -1e30
blocks_per_turn = 4


def start_state(row_count, head_dim):
    return (
        jnp.full((row_count,), negative_floor, jnp.float32),
        jnp.zeros((row_count,), jnp.float32),
        jnp.zeros((row_count, head_dim), jnp.float32),
    )


def fold_scores(partial_value, query_rows, key_rows, value_rows, visible, score_scale):
    running_max, running_sum, weighted = partial_value
    scores = (
        lax.dot_general(
            query_rows, key_rows, (((1,), (1,)), ((), ())), preferred_element_type=jnp.float32
        )
        * score_scale
    )
    masked = jnp.where(visible, scores, negative_floor)
    new_max = jnp.maximum(running_max, jnp.max(masked, axis=1))
    weights = jnp.where(visible, jnp.exp(masked - new_max[:, None]), 0.0)
    rescale = jnp.exp(running_max - new_max)
    running_sum = running_sum * rescale + jnp.sum(weights, axis=1)
    weighted = weighted * rescale[:, None] + jnp.dot(
        weights.astype(jnp.bfloat16), value_rows, preferred_element_type=jnp.float32
    )
    return (new_max, running_sum, weighted)


def attend_blocks(
    partial_value, query_rows, pool_keys, pool_values, block_order, block_count, score_scale
):
    block_len = pool_keys.shape[1]
    head_dim = pool_keys.shape[2]

    def one_turn(turn_number, carried):
        picked = lax.dynamic_slice_in_dim(
            block_order, turn_number * blocks_per_turn, blocks_per_turn
        )
        key_rows = pool_keys[picked].reshape(blocks_per_turn * block_len, head_dim)
        value_rows = pool_values[picked].reshape(blocks_per_turn * block_len, head_dim)
        slots = turn_number * blocks_per_turn + jnp.arange(blocks_per_turn, dtype=jnp.int32)
        visible = jnp.repeat(slots < block_count, block_len)[None, :]
        return fold_scores(carried, query_rows, key_rows, value_rows, visible, score_scale)

    turn_count = (block_count + blocks_per_turn - 1) // blocks_per_turn
    return lax.fori_loop(0, turn_count, one_turn, partial_value)


def active_blocks(block_table, slice_index, which_section, ctx_index, local_pool):
    table_row = block_table[which_section]
    pool_size = table_row.shape[0]
    block_ids = jnp.arange(pool_size, dtype=jnp.int32)
    block_rank = jnp.sum(
        jnp.where(table_row[None, :] == block_ids[:, None], block_ids[None, :], 0), axis=1
    )
    active = block_rank < (slice_index[which_section] + 1) * BPS
    return lax.dynamic_slice_in_dim(active, ctx_index * local_pool, local_pool)


def sorted_blocks(local_live):
    local_pool = local_live.shape[0]
    block_ids = jnp.arange(local_pool, dtype=jnp.int32)
    ranking = jnp.where(local_live, block_ids, local_pool + block_ids)
    block_order = jnp.argsort(ranking)
    return jnp.concatenate([block_order, jnp.zeros((blocks_per_turn,), jnp.int32)])


def on_device(queries, slice_kv, cache_keys, cache_values, block_table, slice_index, out_weight):
    slice_len, heads_here, head_dim = queries.shape
    section_index = lax.axis_index("section")
    ctx_index = lax.axis_index("ctx")
    ctx_count = lax.axis_size("ctx")
    pool_keys = cache_keys[0]
    pool_values = cache_values[0]
    local_pool = pool_keys.shape[0]
    score_scale = 1.0 / math.sqrt(head_dim)
    query_rows = queries.reshape(slice_len * heads_here, head_dim)
    row_count = query_rows.shape[0]
    half_count = slice_len // ctx_count
    own_part = lax.dynamic_slice_in_dim(slice_kv, ctx_index * half_count, half_count, 0)
    token_of_row = jnp.arange(row_count, dtype=jnp.int32) // heads_here
    own_visible = (ctx_index * half_count + jnp.arange(half_count, dtype=jnp.int32))[
        None, :
    ] <= token_of_row[:, None]
    partial_value = fold_scores(
        start_state(row_count, head_dim),
        query_rows,
        own_part[:, 0],
        own_part[:, 1],
        own_visible,
        score_scale,
    )
    local_live = active_blocks(block_table, slice_index, section_index, ctx_index, local_pool)
    block_order = sorted_blocks(local_live)
    block_count = jnp.sum(local_live.astype(jnp.int32))
    partial_value = attend_blocks(
        partial_value, query_rows, pool_keys, pool_values, block_order, block_count, score_scale
    )
    overall_max = lax.pmax(partial_value[0], "ctx")
    factor = jnp.exp(partial_value[0] - overall_max)
    running_sum, weighted = (
        lax.psum((partial_value[1] * factor).astype(jnp.bfloat16), "ctx").astype(jnp.float32),
        lax.psum((partial_value[2] * factor[:, None]).astype(jnp.bfloat16), "ctx").astype(
            jnp.float32
        ),
    )
    attended = (
        (weighted / running_sum[:, None])
        .astype(jnp.bfloat16)
        .reshape(slice_len, heads_here, head_dim)
    )
    projected = jnp.einsum(
        "thd,hdc->tc",
        attended,
        lax.all_gather(out_weight, "section", axis=1, tiled=True),
        preferred_element_type=jnp.float32,
    )
    return lax.psum_scatter(projected.astype(jnp.bfloat16), "head", scatter_dimension=1, tiled=True)


def solution(mesh):
    placed = (
        P(("group", "section"), "head", None),
        P(("group", "section"), None, None),
        P(("group", "section"), "ctx", None, None),
        P(("group", "section"), "ctx", None, None),
        P("group", None),
        P("group"),
        P("head", "section", "ctx"),
    )
    return jax.shard_map(
        on_device,
        mesh=mesh,
        in_specs=placed,
        out_specs=P(("group", "section"), ("ctx", "head")),
        check_vma=False,
    )
```

profile of v0, /device:TPU:9, one launch (start us, length us, event | category | flops | bytes accessed | tf_op | source)
XLA Modules:
  0.0 431.8 jit_solution(7083979972459779517)
XLA Ops:
  7.4 1.2 dynamic_slice.17
  9.4 0.7 add_select_fusion.1
  10.8 1.0 constant_dynamic-slice_fusion.2
  11.9 2.0 fusion.28
  13.9 1.6 copy-done.3
  15.6 0.7 fusion.15
  16.3 0.9 sort.17
  17.2 5.2 %convolution_add_fusion.1 = f32[6144,128]{1,0:T(8,128)} fusion(f32[6144,128]{0,1:T(8,128)} %copy-done.3, f32[6144]{0:T(1024)S(1)} %get-tuple-element.93, f32[6144]{0:T(1024)S(1)} %broadcast_maximum_fusion, s32[6144]{0:T(1024)S(1)} %add_select_fusion, s32[128]{0:T(128)S(1)} %iota_add_fusion, bf16[128,1,128]{2,1,0:T(2,128)(2,1)S(1)} %get-tuple-element.91), kind=kOutput, calls=%fused_computation.21 | convolution fusion | flops 205258752 | bytes 6398464 | tf_op jit(solution)/shard_map/dot_general | solution.py:36
  22.4 17.4 %while.14 = (s32[]{:T(128)}, f32[6144]{0:T(1024)S(1)}, f32[6144]{0:T(1024)S(1)}, f32[6144,128]{1,0:T(8,128)}, s32[]{:T(128)}, /*index=5*/s32[]{:T(128)}, s32[12]...) while((s32[]{:T(128)}, f32[6144]{0:T(1024)S(1)}, ...), condition=%wide.region_8.9_spmd, body=%wide.region_5.8_spmd.sunk | while | flops 1653093376 | bytes 97130800 | solution.py:59
  22.6 0.6 gather_fusion
  23.1 0.6 add_compare_fusion.2
  23.9 2.1 fusion.44
  26.0 3.8 fusion.45
  29.8 0.7 copy-done.1
  30.6 0.6 gather_fusion.1
  31.2 8.7 %convolution_add_fusion.3 = f32[6144,128]{1,0:T(8,128)} fusion(bf16[512,128]{1,0:T(8,128)(2,1)S(1)} %bitcast.47, f32[512,6144]{1,0:T(8,128)} %copy-done.1, f32[6144]{0:T(1024)S(1)} %max.6, pred[512]{0:T(512)(128)(4,1)S(1)} %broadcast_bitcast_fusion.2, f32[6144,128]{1,0:T(8,128)} %get-tuple-element.186, f32[6144]{0:T(1024)S(1)} %get-tuple-element.168), kind=kOutput, calls=%fused_computation.7.clone.1 | convolution fusion | flops 822607872 | bytes 19055104 | tf_op jit(solution)/shard_map/while/body/dot_general | solution.py:36
  39.9 3.9 pmax.7
  43.8 3.3 multiply_convert_fusion
  47.7 3.3 psum.15
  51.0 35.1 %all-reduce.3.cloned.1.call-done = bf16[6144,128]{1,0:T(8,128)(2,1)} async-done(((bf16[6144,128]{1,0:T(8,128)(2,1)}), bf16[6144,128]{1,0:T(8,128)(2,1)}) %all-reduce.3.cloned.1.call-update) | async-done | bytes 1572880 | tf_op jit(solution)/shard_map/psum | solution.py:116
  86.1 2.2 divide_convert_fusion
  88.3 298.8 %all-gather.2.cloned.1.call-done = bf16[24,128,3072]{2,1,0:T(8,128)(2,1)} async-done(((bf16[24,32,3072]{2,1,0:T(8,128)(2,1)}), bf16[24,128,3072]{2,1,0:T(8,128)(2,1)}) %all-gather.2.cloned.1.call-update) | async-done | bytes 18874384 | tf_op jit(solution)/shard_map/all_gather | solution.py:128
  387.1 9.9 %fusion.13 = bf16[256,3072]{1,0:T(8,128)(2,1)} fusion(bf16[24,128,3072]{2,1,0:T(8,128)(2,1)} %all-gather.2.cloned.1.call-done, bf16[256,24,128]{2,1,0:T(8,128)(2,1)S(1)} %bitcast.50), kind=kOutput, calls=%fused_computation.27 | convolution fusion | flops 4832624640 | bytes 22020096 | tf_op jit(solution)/shard_map/thd,hdc->tc/dot_general | solution.py:125
  397.1 27.3 %reduce-scatter.2.cloned.1.call-done = bf16[256,1536]{1,0:T(8,128)(2,1)} async-done(((bf16[256,3072]{1,0:T(8,128)(2,1)}), bf16[256,1536]{1,0:T(8,128)(2,1)}) %reduce-scatter.2.cloned.1.call-update) | async-done | bytes 786448 | tf_op jit(solution)/shard_map/reduce_scatter | solution.py:131
  (33 shorter events, 1.0 us)
Async XLA Ops:
  7.4 1.3 copy-start
  7.4 78.7 %all-reduce.3.cloned.1.call-start = ((), (), s32[]{:S(2)}) async-start(), calls=%async_computation.1 | async-start | bytes 3145728 | tf_op jit(solution)/shard_map/psum | solution.py:116
  13.9 1.7 copy-start.3
  17.2 5.2 %copy-start.2 = (bf16[256,24,128]{2,1,0:T(8,128)(2,1)S(1)}, bf16[256,24,128]{2,1,0:T(8,128)(2,1)}, u32[]{:S(2)}) copy-start(bf16[256,24,128]{2,1,0:T(8,128)(2,1)} %param.9) | copy-start | bytes 4718596
  17.2 5.2 %copy-start.4 = (bf16[1,8,128,128]{3,2,1,0:T(8,128)(2,1)S(1)}, bf16[1,8,128,128]{3,2,1,0:T(8,128)(2,1)}, u32[]{:S(2)}) copy-start(bf16[1,8,128,128]{3,2,1,0:T(8,128)(2,1)} %param.11) | copy-start | bytes 786436
  17.2 5.2 %copy-start.5 = (bf16[1,8,128,128]{3,2,1,0:T(8,128)(2,1)S(1)}, bf16[1,8,128,128]{3,2,1,0:T(8,128)(2,1)}, u32[]{:S(2)}) copy-start(bf16[1,8,128,128]{3,2,1,0:T(8,128)(2,1)} %param.12) | copy-start | bytes 786436
  26.0 4.6 %copy-start.1 = (f32[512,6144]{1,0:T(8,128)}, f32[512,6144]{1,0:T(8,128)S(1)}, u32[]{:S(2)}) copy-start(f32[512,6144]{1,0:T(8,128)S(1)} %get-tuple-element.166) | copy-start | bytes 37748740 | tf_op jit(solution)/shard_map/while
  47.1 340.0 %all-gather.2.cloned.1.call-start = ((), (), s32[]{:S(2)}) async-start(), calls=%async_computation.2 | async-start | bytes 23592960 | tf_op jit(solution)/shard_map/all_gather | solution.py:128
  47.7 376.7 %reduce-scatter.2.cloned.1.call-start = ((), (), s32[]{:S(2)}) async-start(), calls=%async_computation.3 | async-start | bytes 2359296 | tf_op jit(solution)/shard_map/reduce_scatter | solution.py:131
Sparse Core Ops, SparseCore 0:
  47.2 38.8 all-reduce.2
  397.2 27.1 reduce-scatter.1
Sparse Core Ops, SparseCore 1:
  49.2 337.9 all-gather.1
where the time goes:
time: 433 us; the launch traced here: 432 us
  waiting for transfers between devices  362 us (84%)
  matrix products  28 us (6%)
  between operations  16.3 us (4%)
  other arithmetic  12.5 us (3%)
  blocking collectives  7.21 us (2%)
  local copies, waits for them, and re-layouts  5.87 us (1%)
    all_gather x1, waiting for transfers between devices, on_device(): lax.all_gather(out_weight, 'section', axis=1, tiled=True)  299 us
    psum x1, waiting for transfers between devices, on_device(): lax.psum((partial_value[2] * factor[:, None]).astype(jnp.bfloat16), 'ctx')  35.1 us
    reduce_scatter x1, waiting for transfers between devices, on_device(): lax.psum_scatter(projected.astype(jnp.bfloat16), 'head', scatter_dimensio...  27.3 us
    dot_general x2, matrix products, fold_scores(): jnp.dot(weights.astype(jnp.bfloat16), value_rows, preferred_element_type=...  13.9 us
    dot_general x1, matrix products, on_device(): jnp.einsum('thd,hdc->tc', attended, lax.all_gather(out_weight, 'section',...  9.92 us
  transfers between devices with their start and end apart: 3, of which 3 were waited for; matrix products, arithmetic and copies ran while one was open for 1% of the time, Pallas kernels for 0%

commit v1 on v0

v1 whole, which is shorter than its diff:
```python
import functools
import math

import jax
import jax.numpy as jnp
import numpy as np
from jax import lax
from jax.experimental import pallas as pl
from jax.experimental.pallas import tpu as pltpu
from jax.sharding import PartitionSpec as P

BPS = 4
FLOOR = -1.5e30
HIDDEN = -3e38
MESH = pl.DeviceIdType.MESH


def live_keys(block_table, slice_index, block_len, local_pool):
    section = lax.axis_index("section")
    table_row = block_table[section]
    block_ids = jnp.arange(table_row.shape[0], dtype=jnp.int32)
    rank = jnp.sum(
        jnp.where(table_row[None, :] == block_ids[:, None], block_ids[None, :], 0), axis=1
    )
    active = rank < (slice_index[section] + 1) * BPS
    mine = lax.dynamic_slice_in_dim(active, lax.axis_index("ctx") * local_pool, local_pool)
    return jnp.repeat(mine, block_len)


def plain(queries, slice_kv, cache_keys, cache_values, block_table, slice_index, out_weight):
    slice_len, heads, hd = queries.shape
    ctx, nctx = lax.axis_index("ctx"), lax.axis_size("ctx")
    nsec = lax.axis_size("section")
    half = slice_len // nctx
    scale = 1.0 / math.sqrt(hd)
    own = lax.dynamic_slice_in_dim(slice_kv, ctx * half, half, 0)
    keys = jnp.concatenate([cache_keys[0].reshape(-1, hd), own[:, 0]], axis=0)
    values = jnp.concatenate([cache_values[0].reshape(-1, hd), own[:, 1]], axis=0)
    live = live_keys(block_table, slice_index, cache_keys.shape[2], cache_keys.shape[1])
    at = ctx * half + jnp.arange(half, dtype=jnp.int32)
    tokens = jnp.arange(slice_len, dtype=jnp.int32)
    visible = jnp.concatenate(
        [
            jnp.broadcast_to(live[None, :], (slice_len, live.shape[0])),
            at[None, :] <= tokens[:, None],
        ],
        axis=1,
    )

    def one_head(q):
        scores = (
            lax.dot_general(q, keys, (((1,), (1,)), ((), ())), preferred_element_type=jnp.float32)
            * scale
        )
        masked = jnp.where(visible, scores, FLOOR)
        top = jnp.max(masked, axis=1)
        weights = jnp.where(visible, jnp.exp(masked - top[:, None]), 0.0)
        acc = jnp.dot(
            weights.astype(jnp.bfloat16), values, preferred_element_type=jnp.float32
        )
        return top, jnp.sum(weights, axis=1), acc

    top, total, acc = lax.map(one_head, jnp.swapaxes(queries, 0, 1))
    factor = jnp.exp(top - lax.pmax(top, "ctx"))
    total = lax.psum(total * factor, "ctx")
    acc = lax.psum((acc * factor[:, :, None]).astype(jnp.bfloat16), "ctx").astype(jnp.float32)
    attended = jnp.swapaxes((acc / total[:, :, None]).astype(jnp.bfloat16), 0, 1)
    pieces = attended.reshape(slice_len, heads, nsec, hd // nsec).transpose(2, 0, 1, 3)
    pieces = lax.all_to_all(pieces, "section", 0, 0)
    projected = jnp.dot(
        pieces.reshape(nsec * slice_len, -1),
        out_weight.reshape(-1, out_weight.shape[2]),
        preferred_element_type=jnp.float32,
    ).astype(jnp.bfloat16)
    summed = lax.psum_scatter(projected, "head", scatter_dimension=1, tiled=True)
    return lax.psum_scatter(summed, "section", scatter_dimension=0, tiled=True)


def kernel(
    dims,
    q_ref, ck_ref, cv_ref, sk_ref, sv_ref, bias_ref, perm_ref, w_ref,
    out_ref,
    w_all, a_all, a_send, acc_own, acc_send, acc_recv, st_own, st_send, st_recv, c_send, c_recv,
    w_local, w_sems, acc_sems, st_sems, z_send, z_recv, x_sems, core_send, core_recv, c_ssem, c_rsem,
):
    slice_len, heads, hd, nsec, stages = dims
    half = slice_len // 2
    per_stage = heads // stages
    group_count = per_stage // nsec
    width = per_stage * hd
    kcols = group_count * hd
    ncols = out_ref.shape[1]
    g, s = lax.axis_index("group"), lax.axis_index("section")
    c, h = lax.axis_index("ctx"), lax.axis_index("head")
    core_peer = (g, s, 1 - c, h)
    x_peer = (g, s, c, 1 - h)

    def sec(k):
        return lax.rem(s + k, nsec)

    def z_peer(k):
        return (g, sec(k), c, h)

    def remote(src, dst, ssem, rsem, to):
        return pltpu.make_async_remote_copy(
            src_ref=src, dst_ref=dst, send_sem=ssem, recv_sem=rsem,
            device_id=to, device_id_type=MESH,
        )

    barrier = pltpu.get_barrier_semaphore()
    for peer in [core_peer, x_peer] + [z_peer(k) for k in range(1, nsec)]:
        pl.semaphore_signal(barrier, inc=1, device_id=peer, device_id_type=MESH)
    pl.semaphore_wait(barrier, nsec + 1)

    def cols_of(which):
        return pl.ds(pl.multiple_of(which * ncols, 128), ncols)

    w_own = pltpu.make_async_copy(w_ref.at[:, cols_of(h)], w_all.at[h], w_local)
    w_own.start()
    w_swap = remote(w_ref.at[:, cols_of(1 - h)], w_all.at[h], w_sems.at[0], w_sems.at[1], x_peer)
    w_swap.start()

    scale = math.log2(math.e) / math.sqrt(hd)
    own_at = pl.ds(pl.multiple_of(c * half, 128), half)
    sends = [w_swap]
    lane = lax.broadcasted_iota(jnp.int32, (half, 128), 1)
    mine = pl.ds(pl.multiple_of(c * half, 128), half)
    theirs = pl.ds(pl.multiple_of((1 - c) * half, 128), half)
    nt = (((1,), (1,)), ((), ()))

    def attend(st):
        st_own[st] = jnp.zeros((half, 128), jnp.float32)
        st_send[st] = jnp.zeros((half, 128), jnp.float32)

        def one(j, rows_at, acc_store, st_ref, row0):
            at = pl.multiple_of((st * per_stage + j) * hd, 128)
            q = q_ref[rows_at, pl.ds(at, hd)]
            t1 = (
                lax.dot_general(q, ck_ref[...], nt, preferred_element_type=jnp.float32) * scale
                + bias_ref[...]
            )
            t2 = (
                lax.dot_general(
                    q, sk_ref[own_at, :], nt, preferred_element_type=jnp.float32
                )
                * scale
            )
            row = lax.broadcasted_iota(jnp.int32, (half, half), 0) + row0
            col = lax.broadcasted_iota(jnp.int32, (half, half), 1) + c * half
            t2 = jnp.where(row >= col, t2, HIDDEN)
            top = jnp.maximum(
                jnp.max(t1, axis=1, keepdims=True), jnp.max(t2, axis=1, keepdims=True)
            )
            top = jnp.maximum(top, FLOOR)
            p1, p2 = jnp.exp2(t1 - top), jnp.exp2(t2 - top)
            total = jnp.sum(p1, axis=1, keepdims=True) + jnp.sum(p2, axis=1, keepdims=True)
            acc = jnp.dot(
                p1.astype(jnp.bfloat16), cv_ref[...], preferred_element_type=jnp.float32
            ) + jnp.dot(
                p2.astype(jnp.bfloat16), sv_ref[own_at, :], preferred_element_type=jnp.float32
            )
            acc_store(pl.multiple_of(j * hd, 128), acc)
            old = st_ref[st]
            st_ref[st] = jnp.where(lane == j, top, jnp.where(lane == 64 + j, total, old))

        def keep(at, acc):
            acc_own[st, :, pl.ds(at, hd)] = acc

        def give(at, acc):
            acc_send[st, :, pl.ds(at, hd)] = acc.astype(jnp.bfloat16)

        def body(j, carry):
            one(j, theirs, give, st_send, (1 - c) * half)
            one(j, mine, keep, st_own, c * half)
            return carry

        lax.fori_loop(0, per_stage, body, 0)
        for buf, got, sems in ((acc_send, acc_recv, acc_sems), (st_send, st_recv, st_sems)):
            copy = remote(buf.at[st], got.at[st], sems.at[0, st], sems.at[1, st], core_peer)
            copy.start()
            sends.append(copy)

    def merge(st):
        for buf, got, sems in ((acc_send, acc_recv, acc_sems), (st_send, st_recv, st_sems)):
            remote(buf.at[st], got.at[st], sems.at[0, st], sems.at[1, st], core_peer).wait_recv()
        stat0, stat1 = st_own[st], st_recv[st]
        done = []
        for j in range(per_stage):
            top0, top1 = stat0[:, j : j + 1], stat1[:, j : j + 1]
            top = jnp.maximum(top0, top1)
            f0, f1 = jnp.exp2(top0 - top), jnp.exp2(top1 - top)
            inv = 1.0 / (stat0[:, 64 + j : 65 + j] * f0 + stat1[:, 64 + j : 65 + j] * f1)
            acc0 = acc_own[st, :, j * hd : (j + 1) * hd]
            acc1 = acc_recv[st, :, j * hd : (j + 1) * hd].astype(jnp.float32)
            done.append(((acc0 * (f0 * inv)) + (acc1 * (f1 * inv))).astype(jnp.bfloat16))
        for i in range(group_count):
            rows = jnp.concatenate(done[i * nsec : (i + 1) * nsec], axis=1)
            moved = jnp.dot(rows, perm_ref[...], preferred_element_type=jnp.float32).astype(
                jnp.bfloat16
            )
            for k in range(nsec):
                a_send[st, k, :, i * hd : (i + 1) * hd] = moved[:, k * hd : (k + 1) * hd]
        a_all[st, h, c, s] = a_send[st, s]
        for k in range(1, nsec):
            copy = remote(
                a_send.at[st, sec(k)], a_all.at[st, h, c, s],
                z_send.at[st, k - 1], z_recv.at[st, k - 1], z_peer(k),
            )
            copy.start()
            sends.append(copy)

    def forward(st):
        for k in range(1, nsec):
            remote(
                a_send.at[st, 0], a_all.at[st, h, c, sec(nsec - k)],
                z_send.at[st, k - 1], z_recv.at[st, k - 1], z_peer(k),
            ).wait_recv()
        held = a_all.at[st, h, c]
        for copy in (
            remote(held, held, x_sems.at[0, st], x_sems.at[1, st], x_peer),
            remote(held, held, core_send.at[st, 0], core_recv.at[st, 0], core_peer),
        ):
            copy.start()
            sends.append(copy)

    def share(st):
        held = a_all.at[st, 1 - h, c]
        remote(held, held, x_sems.at[0, st], x_sems.at[1, st], x_peer).wait_recv()
        copy = remote(held, held, core_send.at[st, 1], core_recv.at[st, 1], core_peer)
        copy.start()
        sends.append(copy)

    for step in range(stages + 3):
        if step < stages:
            attend(step)
        if 1 <= step <= stages:
            merge(step - 1)
        if 2 <= step <= stages + 1:
            forward(step - 2)
        if 3 <= step:
            share(step - 3)

    w_own.wait()
    w_swap_in = remote(w_ref.at[:, cols_of(h)], w_all.at[1 - h], w_sems.at[0], w_sems.at[1], x_peer)
    w_swap_in.wait_recv()
    for st in range(stages):
        for i, which in enumerate((h, 1 - h)):
            held = a_all.at[st, which, 1 - c]
            remote(held, held, core_send.at[st, i], core_recv.at[st, i], core_peer).wait_recv()

    tile = 512 if ncols % 512 == 0 else 128

    def product(which, store):
        def body(n, carry):
            at = pl.ds(pl.multiple_of(n * tile, 128), tile)
            total = jnp.zeros((slice_len, tile), jnp.float32)
            for hh in range(2):
                for st in range(stages):
                    left = a_all[st, hh, :, which].reshape(slice_len, kcols)
                    total += jnp.dot(
                        left,
                        w_all[hh, st * kcols : (st + 1) * kcols, at],
                        preferred_element_type=jnp.float32,
                    )
            store(at, total)
            return carry

        lax.fori_loop(0, ncols // tile, body, 0)

    for k in range(1, nsec):
        def put(at, total, k=k):
            c_send[k - 1, :, at] = total.astype(jnp.bfloat16)

        product(sec(k), put)
        copy = remote(
            c_send.at[k - 1], c_recv.at[k - 1], c_ssem.at[k - 1], c_rsem.at[k - 1], z_peer(k)
        )
        copy.start()
        sends.append(copy)

    for k in range(1, nsec):
        remote(
            c_send.at[k - 1], c_recv.at[k - 1], c_ssem.at[k - 1], c_rsem.at[k - 1], z_peer(k)
        ).wait_recv()

    def finish(at, total):
        for k in range(1, nsec):
            total += c_recv[k - 1, :, at].astype(jnp.float32)
        out_ref[:, at] = total.astype(jnp.bfloat16)

    product(s, finish)
    for copy in sends:
        copy.wait_send()


def fused(queries, slice_kv, cache_keys, cache_values, block_table, slice_index, out_weight):
    slice_len, heads, hd = queries.shape
    nsec = lax.axis_size("section")
    stages = 3
    half = slice_len // 2
    per_stage = heads // stages
    width = per_stage * hd
    kcols = per_stage // nsec * hd
    ncols = out_weight.shape[2] // 2
    depth = out_weight.shape[0] * out_weight.shape[1]
    live = live_keys(block_table, slice_index, cache_keys.shape[2], cache_keys.shape[1])
    bias = jnp.where(live, 0.0, HIDDEN).astype(jnp.float32)[None, :]
    piece = hd // nsec
    perm = np.zeros((nsec, nsec, piece, nsec, nsec, piece), np.float32)
    for head in range(nsec):
        for part in range(nsec):
            for r in range(piece):
                perm[head, part, r, part, head, r] = 1.0
    perm = jnp.asarray(perm.reshape(nsec * hd, nsec * hd), jnp.bfloat16)
    bf16, f32 = jnp.bfloat16, jnp.float32
    dma = pltpu.SemaphoreType.DMA
    vmem = pl.BlockSpec(memory_space=pltpu.VMEM)
    return pl.pallas_call(
        functools.partial(kernel, (slice_len, heads, hd, nsec, stages)),
        out_shape=jax.ShapeDtypeStruct((slice_len, ncols), bf16),
        in_specs=[vmem] * 7 + [pl.BlockSpec(memory_space=pl.ANY)],
        out_specs=vmem,
        scratch_shapes=[
            pltpu.VMEM((2, depth, ncols), bf16),
            pltpu.VMEM((stages, 2, 2, nsec, half, kcols), bf16),
            pltpu.VMEM((stages, nsec, half, kcols), bf16),
            pltpu.VMEM((stages, half, width), f32),
            pltpu.VMEM((stages, half, width), bf16),
            pltpu.VMEM((stages, half, width), bf16),
            pltpu.VMEM((stages, half, 128), f32),
            pltpu.VMEM((stages, half, 128), f32),
            pltpu.VMEM((stages, half, 128), f32),
            pltpu.VMEM((nsec - 1, slice_len, ncols), bf16),
            pltpu.VMEM((nsec - 1, slice_len, ncols), bf16),
            dma,
            dma((2,)),
            dma((2, stages)),
            dma((2, stages)),
            dma((stages, nsec - 1)),
            dma((stages, nsec - 1)),
            dma((2, stages)),
            dma((stages, 2)),
            dma((stages, 2)),
            dma((nsec - 1,)),
            dma((nsec - 1,)),
        ],
        compiler_params=pltpu.CompilerParams(
            collective_id=0, has_side_effects=True, vmem_limit_bytes=52 * 1024 * 1024
        ),
    )(
        queries.reshape(slice_len, heads * hd),
        cache_keys.reshape(-1, hd),
        cache_values.reshape(-1, hd),
        slice_kv[:, 0],
        slice_kv[:, 1],
        bias,
        perm,
        out_weight.reshape(depth, -1),
    )


def on_device(*arrays):
    slice_len, heads, hd = arrays[0].shape
    nsec = lax.axis_size("section")
    fits = (
        lax.axis_size("ctx") == 2
        and lax.axis_size("head") == 2
        and hd == 128
        and slice_len % 256 == 0
        and heads % (3 * nsec) == 0
        and heads // 3 <= 64
        and arrays[6].shape[2] % 256 == 0
    )
    return fused(*arrays) if fits else plain(*arrays)


def solution(mesh):
    placed = (
        P(("group", "section"), "head", None),
        P(("group", "section"), None, None),
        P(("group", "section"), "ctx", None, None),
        P(("group", "section"), "ctx", None, None),
        P("group", None),
        P("group"),
        P("head", "section", "ctx"),
    )
    return jax.shard_map(
        on_device,
        mesh=mesh,
        in_specs=placed,
        out_specs=P(("group", "section"), ("ctx", "head")),
        check_vma=False,
    )
```

time: 433 us -> 156 us (0.36)
  waiting for transfers between devices: 362 us -> 0 us
  Pallas kernels: 0 us -> 148 us
  matrix products: 28 us -> 0 us
  between operations: 16.3 us -> 0.72 us
  other arithmetic: 12.5 us -> 0.2 us
  blocking collectives: 7.21 us -> 0 us
    all_gather x1 -> x0, waiting for transfers between devices: 299 us -> none  [on_device(): lax.all_gather(out_weight, 'section', axis=1, tiled=True)]
    pallas_call x0 -> x1, Pallas kernels: none -> 148 us  [fused(): pl.pallas_call(functools.partial(kernel, (slice_len, heads, hd, nsec, sta...]
    psum x1 -> x0, waiting for transfers between devices: 35.1 us -> none  [on_device(): lax.psum((partial_value[2] * factor[:, None]).astype(jnp.bfloat16), 'ctx')]
    dot_general x5 -> x0, matrix products: 28 us -> none  [the longest x2 13.9 us: fold_scores(): jnp.dot(weights.astype(jnp.bfloat16), value_rows, preferred_element_type=...]
    reduce_scatter x1 -> x0, waiting for transfers between devices: 27.3 us -> none  [on_device(): lax.psum_scatter(projected.astype(jnp.bfloat16), 'head', scatter_dimensio...]
    convert_element_type x4 -> x0, other arithmetic: 5.48 us -> none  [the longest x1 3.26 us: on_device(): (partial_value[2] * factor[:, None]).astype(jnp.bfloat16)]
    reduce_sum x3 -> x1, other arithmetic: 4.62 us -> 0.11 us  [live_keys(): jnp.sum(jnp.where(table_row[None, :] == block_ids[:, None], block_ids[Non...]
  transfers between devices with their start and end apart: 3 -> 0, of which waited for: 3 -> 0; matrix products, arithmetic and copies ran while one was open for 1% -> 0% of each run, Pallas kernels for 0% -> 0%
where the time goes in v1:
time: 156 us
  Pallas kernels  148 us (95%)
  local copies, waits for them, and re-layouts  6.44 us (4%)
    pallas_call x1, Pallas kernels, fused(): pl.pallas_call(functools.partial(kernel, (slice_len, heads, hd, nsec, sta...  148 us
    unnamed x10, local copies, waits for them, and re-layouts  3.88 us

profile of v1, /device:TPU:9, one launch (start us, length us, event | category | flops | bytes accessed | tf_op | source)
XLA Modules:
  0.0 155.6 jit_solution(266941898813851204)
XLA Ops:
  0.0 0.0 copy-start
  0.0 1.2 dynamic_slice.10
  1.9 0.0 copy-done
  1.9 0.1 select_reduce_fusion
  2.1 0.1 dynamic-slice_select_fusion
  2.1 0.1 broadcast_in_dim.30
  2.2 1.2 fusion
  3.5 0.0 copy-start.1
  3.5 0.0 copy-start.2
  3.5 0.0 copy-start.3
  3.5 3.0 %copy.19 = bf16[32,8,24,128]{3,1,2,0:T(8,128)(2,1)} copy(bf16[32,8,24,128]{3,2,1,0:T(8,128)(2,1)} %bitcast.20) | data formatting | bytes 3145728
  6.5 0.0 copy-done.1
  6.5 0.0 copy-done.2
  6.5 0.0 copy-done.3
  6.5 148.2 %shard_map.82 = bf16[256,1536]{1,0:T(8,128)(2,1)S(1)} custom-call(bf16[256,3072]{1,0:T(8,128)(2,1)} %bitcast.18, bf16[1024,128]{1,0:T(8,128)(2,1)S(1)} %bitcast.15, bf16[1024,128]{1,0:T(8,128)(2,1)S(1)} %bitcast.16, bf16[256,128]{1,0:T(8,128)(2,1)S(1)} %get-tuple-element.8.sk_ref, bf16[256,128]{1,0:T(8,128)(2,1)S(1)} %get-tuple-element.7.sv_ref, ...), custom_call_target="tpu_custom_call" | custom-call | tf_op jit(solution)/shard_map/pallas_call | solution.py:318
  154.7 0.9 copy.21
  (3 shorter events, 0.0 us)
Async XLA Ops:
  0.0 1.9 %copy-start = (s32[4,16]{1,0:T(4,128)S(1)}, s32[4,16]{1,0:T(4,128)}, u32[]{:S(2)}) copy-start(s32[4,16]{1,0:T(4,128)} %param.12) | copy-start | bytes 772
  3.5 3.0 %copy-start.1 = (bf16[512,512]{1,0:T(8,128)(2,1)S(1)}, bf16[512,512]{1,0:T(8,128)(2,1)}, u32[]{:S(2)}) copy-start(bf16[512,512]{1,0:T(8,128)(2,1)} %constant.28.clone.perm_ref) | copy-start | bytes 1572868
  3.5 3.0 %copy-start.2 = (bf16[1,8,128,128]{3,2,1,0:T(8,128)(2,1)S(1)}, bf16[1,8,128,128]{3,2,1,0:T(8,128)(2,1)}, u32[]{:S(2)}) copy-start(bf16[1,8,128,128]{3,2,1,0:T(8,128)(2,1)} %param.10) | copy-start | bytes 786436
  3.5 3.0 %copy-start.3 = (bf16[1,8,128,128]{3,2,1,0:T(8,128)(2,1)S(1)}, bf16[1,8,128,128]{3,2,1,0:T(8,128)(2,1)}, u32[]{:S(2)}) copy-start(bf16[1,8,128,128]{3,2,1,0:T(8,128)(2,1)} %param.11) | copy-start | bytes 786436

commit v2 on v1

--- a/solution.py
+++ b/solution.py
@@ -80,8 +80,10 @@
     dims,
     q_ref, ck_ref, cv_ref, sk_ref, sv_ref, bias_ref, perm_ref, w_ref,
     out_ref,
-    w_all, a_all, a_send, acc_own, acc_send, acc_recv, st_own, st_send, st_recv, c_send, c_recv,
-    w_local, w_sems, acc_sems, st_sems, z_send, z_recv, x_sems, core_send, core_recv, c_ssem, c_rsem,
+    w_all, a_all, a_send, acc_own, acc_send, acc_recv, st_own, st_send, st_recv,
+    right_send, right_recv, left_send, left_recv, kept,
+    w_local, w_sems, acc_sems, st_sems, z_send, z_recv, x_sems, core_send, core_recv,
+    r_ssem, r_rsem, l_ssem, l_rsem,
 ):
     slice_len, heads, hd, nsec, stages = dims
     half = slice_len // 2
@@ -93,6 +95,7 @@
     g, s = lax.axis_index("group"), lax.axis_index("section")
     c, h = lax.axis_index("ctx"), lax.axis_index("head")
     core_peer = (g, s, 1 - c, h)
+    twin = (1 - g, s, c, h)
     x_peer = (g, s, c, 1 - h)
 
     def sec(k):
@@ -108,21 +111,38 @@
         )
 
     barrier = pltpu.get_barrier_semaphore()
-    for peer in [core_peer, x_peer] + [z_peer(k) for k in range(1, nsec)]:
+    for peer in [core_peer, x_peer, twin] + [z_peer(k) for k in range(1, nsec)]:
         pl.semaphore_signal(barrier, inc=1, device_id=peer, device_id_type=MESH)
-    pl.semaphore_wait(barrier, nsec + 1)
+    pl.semaphore_wait(barrier, nsec + 2)
 
     def cols_of(which):
         return pl.ds(pl.multiple_of(which * ncols, 128), ncols)
 
     w_own = pltpu.make_async_copy(w_ref.at[:, cols_of(h)], w_all.at[h], w_local)
     w_own.start()
-    w_swap = remote(w_ref.at[:, cols_of(1 - h)], w_all.at[h], w_sems.at[0], w_sems.at[1], x_peer)
-    w_swap.start()
+    depth = w_ref.shape[0]
+    w_rows = depth // (2 * stages)
+
+    def w_at(which, i):
+        return pl.ds(pl.multiple_of(which * (depth // 2) + i * w_rows, 16), w_rows)
+
+    def w_swap(i):
+        return remote(
+            w_ref.at[w_at(g, i), cols_of(1 - h)], w_all.at[h, w_at(g, i)],
+            w_sems.at[0, i], w_sems.at[1, i], x_peer,
+        )
+
+    def w_pass(i):
+        held = w_all.at[1 - h, w_at(g, i)]
+        return remote(held, held, w_sems.at[2, i], w_sems.at[3, i], twin)
+
+    swaps = [w_swap(i) for i in range(stages)]
+    for copy in swaps:
+        copy.start()
 
     scale = math.log2(math.e) / math.sqrt(hd)
     own_at = pl.ds(pl.multiple_of(c * half, 128), half)
-    sends = [w_swap]
+    sends = list(swaps)
     lane = lax.broadcasted_iota(jnp.int32, (half, 128), 1)
     mine = pl.ds(pl.multiple_of(c * half, 128), half)
     theirs = pl.ds(pl.multiple_of((1 - c) * half, 128), half)
@@ -235,60 +255,99 @@
             attend(step)
         if 1 <= step <= stages:
             merge(step - 1)
+        if 1 <= step <= stages:
+            w_swap(step - 1).wait_recv()
+            copy = w_pass(step - 1)
+            copy.start()
+            sends.append(copy)
         if 2 <= step <= stages + 1:
             forward(step - 2)
         if 3 <= step:
             share(step - 3)
 
     w_own.wait()
-    w_swap_in = remote(w_ref.at[:, cols_of(h)], w_all.at[1 - h], w_sems.at[0], w_sems.at[1], x_peer)
-    w_swap_in.wait_recv()
+    for i in range(stages):
+        w_pass(i).wait_recv()
     for st in range(stages):
         for i, which in enumerate((h, 1 - h)):
             held = a_all.at[st, which, 1 - c]
             remote(held, held, core_send.at[st, i], core_recv.at[st, i], core_peer).wait_recv()
 
-    tile = 512 if ncols % 512 == 0 else 128
-
-    def product(which, store):
-        def body(n, carry):
-            at = pl.ds(pl.multiple_of(n * tile, 128), tile)
-            total = jnp.zeros((slice_len, tile), jnp.float32)
-            for hh in range(2):
-                for st in range(stages):
-                    left = a_all[st, hh, :, which].reshape(slice_len, kcols)
-                    total += jnp.dot(
-                        left,
-                        w_all[hh, st * kcols : (st + 1) * kcols, at],
-                        preferred_element_type=jnp.float32,
-                    )
-            store(at, total)
-            return carry
-
-        lax.fori_loop(0, ncols // tile, body, 0)
-
-    for k in range(1, nsec):
-        def put(at, total, k=k):
-            c_send[k - 1, :, at] = total.astype(jnp.bfloat16)
-
-        product(sec(k), put)
-        copy = remote(
-            c_send.at[k - 1], c_recv.at[k - 1], c_ssem.at[k - 1], c_rsem.at[k - 1], z_peer(k)
-        )
-        copy.start()
-        sends.append(copy)
-
-    for k in range(1, nsec):
-        remote(
-            c_send.at[k - 1], c_recv.at[k - 1], c_ssem.at[k - 1], c_rsem.at[k - 1], z_peer(k)
-        ).wait_recv()
-
-    def finish(at, total):
-        for k in range(1, nsec):
-            total += c_recv[k - 1, :, at].astype(jnp.float32)
-        out_ref[:, at] = total.astype(jnp.bfloat16)
-
-    product(s, finish)
+    chunk = right_send.shape[2]
+    chunks = ncols // chunk
+
+    def product(which, n):
+        at = pl.ds(pl.multiple_of(n * chunk, 128), chunk)
+        total = jnp.zeros((slice_len, chunk), jnp.float32)
+        for hh in range(2):
+            for st in range(stages):
+                left = a_all[st, hh, :, which].reshape(slice_len, kcols)
+                total += jnp.dot(
+                    left,
+                    w_all[hh, st * kcols : (st + 1) * kcols, at],
+                    preferred_element_type=jnp.float32,
+                )
+        return total
+
+    last = nsec - 1
+    ways = (
+        (right_send, right_recv, r_ssem, r_rsem, s, 1, lambda i: last - i),
+        (left_send, left_recv, l_ssem, l_rsem, last - s, -1, lambda i: i),
+    )
+
+    def hop(way, m):
+        out, got, ssem, rsem, _, step, _ = way
+        to = (g, jnp.clip(s + step, 0, last), c, h)
+        return remote(out.at[m], got.at[m], ssem.at[m], rsem.at[m], to)
+
+    def wave(t, carry):
+        for way in ways:
+            out, got, _, _, behind, _, owner = way
+            m = t - behind
+
+            @pl.when((m >= 0) & (m < chunks * (last - behind)))
+            def _():
+                total = product(owner(m // chunks), m % chunks)
+
+                @pl.when(behind == 0)
+                def _():
+                    out[m] = total.astype(jnp.bfloat16)
+
+                @pl.when(behind > 0)
+                def _():
+                    hop(way, m).wait_recv()
+                    out[m] = (total + got[m].astype(jnp.float32)).astype(jnp.bfloat16)
+
+                @pl.when(m >= 2)
+                def _():
+                    hop(way, m - 2).wait_send()
+
+                hop(way, m).start()
+
+        return carry
+
+    lax.fori_loop(0, chunks * last + last, wave, 0)
+
+    for n in range(chunks):
+        kept[...] = product(s, n)
+        for way in ways:
+            got, behind = way[1], way[4]
+            m = (last - behind) * chunks + n
+
+            @pl.when(behind > 0)
+            def _():
+                hop(way, m).wait_recv()
+                kept[...] += got[m].astype(jnp.float32)
+
+        out_ref[:, n * chunk : (n + 1) * chunk] = kept[...].astype(jnp.bfloat16)
+    for way in ways:
+        count = chunks * (last - way[4])
+        for back in (2, 1):
+
+            @pl.when(count >= back)
+            def _():
+                hop(way, count - back).wait_send()
+
     for copy in sends:
         copy.wait_send()
 
@@ -303,6 +362,8 @@
     kcols = per_stage // nsec * hd
     ncols = out_weight.shape[2] // 2
     depth = out_weight.shape[0] * out_weight.shape[1]
+    chunk = 512 if ncols % 512 == 0 else 128
+    items = (nsec - 1) * (ncols // chunk)
     live = live_keys(block_table, slice_index, cache_keys.shape[2], cache_keys.shape[1])
     bias = jnp.where(live, 0.0, HIDDEN).astype(jnp.float32)[None, :]
     piece = hd // nsec
@@ -330,10 +391,10 @@
             pltpu.VMEM((stages, half, 128), f32),
             pltpu.VMEM((stages, half, 128), f32),
             pltpu.VMEM((stages, half, 128), f32),
-            pltpu.VMEM((nsec - 1, slice_len, ncols), bf16),
-            pltpu.VMEM((nsec - 1, slice_len, ncols), bf16),
+            *[pltpu.VMEM((items, slice_len, chunk), bf16)] * 4,
+            pltpu.VMEM((slice_len, chunk), f32),
             dma,
-            dma((2,)),
+            dma((4, stages)),
             dma((2, stages)),
             dma((2, stages)),
             dma((stages, nsec - 1)),
@@ -341,8 +402,7 @@
             dma((2, stages)),
             dma((stages, 2)),
             dma((stages, 2)),
-            dma((nsec - 1,)),
-            dma((nsec - 1,)),
+            *[dma((items,))] * 4,
         ],
         compiler_params=pltpu.CompilerParams(
             collective_id=0, has_side_effects=True, vmem_limit_bytes=52 * 1024 * 1024
@@ -365,6 +425,8 @@
     fits = (
         lax.axis_size("ctx") == 2
         and lax.axis_size("head") == 2
+        and lax.axis_size("group") == 2
+        and arrays[6].shape[0] * arrays[6].shape[1] % 96 == 0
         and hd == 128
         and slice_len % 256 == 0
         and heads % (3 * nsec) == 0

time: 156 us -> 113 us (0.72); the launches traced: 156 us -> 111 us
  Pallas kernels: 148 us -> 103 us
    pallas_call x1, Pallas kernels: 148 us -> 103 us  [fused(): pl.pallas_call(functools.partial(kernel, (slice_len, heads, hd, nsec, sta...]
where the time goes in v2:
time: 113 us; the launch traced here: 111 us
  Pallas kernels  103 us (91%)
  local copies, waits for them, and re-layouts  6.44 us (6%)
    pallas_call x1, Pallas kernels, fused(): pl.pallas_call(functools.partial(kernel, (slice_len, heads, hd, nsec, sta...  103 us
    unnamed x10, local copies, waits for them, and re-layouts  3.88 us

profile of v2, /device:TPU:9, one launch (start us, length us, event | category | flops | bytes accessed | tf_op | source)
XLA Modules:
  0.0 110.8 jit_solution(13225611334274311004)
XLA Ops:
  0.0 0.0 copy-start
  0.0 1.2 %dynamic_slice.10 = s32[1]{0:T(128)} dynamic-slice(s32[4]{0:T(128)} %param.13, s32[]{:T(128)S(6)} %select_n.26), dynamic_slice_sizes={1} | dynamic-slice | bytes 12 | tf_op jit(solution)/shard_map/dynamic_slice | solution.py:25
  1.9 0.0 copy-done
  1.9 0.1 select_reduce_fusion
  2.1 0.1 dynamic-slice_select_fusion
  2.1 0.1 broadcast_in_dim.30
  2.2 1.2 %fusion = (bf16[256,1,128]{2,1,0:T(2,128)(2,1)S(1)}, bf16[256,1,128]{2,1,0:T(2,128)(2,1)S(1)}) fusion(bf16[256,2,128]{2,1,0:T(2,128)(2,1)} %param.9), kind=kLoop, calls=%fused_computation.8 | loop fusion | bytes 262144 | tf_op jit(solution)/shard_map/slice | solution.py:415
  3.5 0.0 copy-start.1
  3.5 0.0 copy-start.2
  3.5 0.0 copy-start.3
  3.5 3.0 %copy.19 = bf16[32,8,24,128]{3,1,2,0:T(8,128)(2,1)} copy(bf16[32,8,24,128]{3,2,1,0:T(8,128)(2,1)} %bitcast.20) | data formatting | bytes 3145728
  6.5 0.0 copy-done.1
  6.5 0.0 copy-done.2
  6.5 0.0 copy-done.3
  6.5 103.5 %shard_map.82 = bf16[256,1536]{1,0:T(8,128)(2,1)S(1)} custom-call(bf16[256,3072]{1,0:T(8,128)(2,1)} %bitcast.18, bf16[1024,128]{1,0:T(8,128)(2,1)S(1)} %bitcast.15, bf16[1024,128]{1,0:T(8,128)(2,1)S(1)} %bitcast.16, bf16[256,128]{1,0:T(8,128)(2,1)S(1)} %get-tuple-element.8.sk_ref, bf16[256,128]{1,0:T(8,128)(2,1)S(1)} %get-tuple-element.7.sv_ref, ...), custom_call_target="tpu_custom_call" | custom-call | tf_op jit(solution)/shard_map/pallas_call | solution.py:379
  110.0 0.9 copy.21
  (3 shorter events, 0.0 us)
Async XLA Ops:
  0.0 1.9 %copy-start = (s32[4,16]{1,0:T(4,128)S(1)}, s32[4,16]{1,0:T(4,128)}, u32[]{:S(2)}) copy-start(s32[4,16]{1,0:T(4,128)} %param.12) | copy-start | bytes 772
  3.5 3.0 %copy-start.1 = (bf16[512,512]{1,0:T(8,128)(2,1)S(1)}, bf16[512,512]{1,0:T(8,128)(2,1)}, u32[]{:S(2)}) copy-start(bf16[512,512]{1,0:T(8,128)(2,1)} %constant.28.clone.perm_ref) | copy-start | bytes 1572868
  3.5 3.0 %copy-start.2 = (bf16[1,8,128,128]{3,2,1,0:T(8,128)(2,1)S(1)}, bf16[1,8,128,128]{3,2,1,0:T(8,128)(2,1)}, u32[]{:S(2)}) copy-start(bf16[1,8,128,128]{3,2,1,0:T(8,128)(2,1)} %param.10) | copy-start | bytes 786436
  3.5 3.0 %copy-start.3 = (bf16[1,8,128,128]{3,2,1,0:T(8,128)(2,1)S(1)}, bf16[1,8,128,128]{3,2,1,0:T(8,128)(2,1)}, u32[]{:S(2)}) copy-start(bf16[1,8,128,128]{3,2,1,0:T(8,128)(2,1)} %param.11) | copy-start | bytes 786436

commit v3 on v2

--- a/solution.py
+++ b/solution.py
@@ -87,11 +87,12 @@
 ):
     slice_len, heads, hd, nsec, stages = dims
     half = slice_len // 2
-    per_stage = heads // stages
-    group_count = per_stage // nsec
-    width = per_stage * hd
-    kcols = group_count * hd
+    rows = half // stages
+    tokens = 2 * rows
+    group_count = heads // nsec
     ncols = out_ref.shape[1]
+    batch = 4
+    blocks = heads // batch
     g, s = lax.axis_index("group"), lax.axis_index("section")
     c, h = lax.axis_index("ctx"), lax.axis_index("head")
     core_peer = (g, s, 1 - c, h)
@@ -121,7 +122,8 @@
     w_own = pltpu.make_async_copy(w_ref.at[:, cols_of(h)], w_all.at[h], w_local)
     w_own.start()
     depth = w_ref.shape[0]
-    w_rows = depth // (2 * stages)
+    parts = w_sems.shape[1]
+    w_rows = depth // (2 * parts)
 
     def w_at(which, i):
         return pl.ds(pl.multiple_of(which * (depth // 2) + i * w_rows, 16), w_rows)
@@ -136,25 +138,20 @@
         held = w_all.at[1 - h, w_at(g, i)]
         return remote(held, held, w_sems.at[2, i], w_sems.at[3, i], twin)
 
-    swaps = [w_swap(i) for i in range(stages)]
+    swaps = [w_swap(i) for i in range(parts)]
     for copy in swaps:
         copy.start()
 
     scale = math.log2(math.e) / math.sqrt(hd)
     own_at = pl.ds(pl.multiple_of(c * half, 128), half)
     sends = list(swaps)
-    lane = lax.broadcasted_iota(jnp.int32, (half, 128), 1)
-    mine = pl.ds(pl.multiple_of(c * half, 128), half)
-    theirs = pl.ds(pl.multiple_of((1 - c) * half, 128), half)
+    lane = lax.broadcasted_iota(jnp.int32, (rows, 128), 1)
     nt = (((1,), (1,)), ((), ()))
 
-    def attend(st):
-        st_own[st] = jnp.zeros((half, 128), jnp.float32)
-        st_send[st] = jnp.zeros((half, 128), jnp.float32)
-
-        def one(j, rows_at, acc_store, st_ref, row0):
-            at = pl.multiple_of((st * per_stage + j) * hd, 128)
-            q = q_ref[rows_at, pl.ds(at, hd)]
+    def attend(st, first, end):
+        def one(j, core, acc_store, st_ref):
+            row0 = pl.multiple_of(st * tokens + core * rows, 16)
+            q = q_ref[pl.ds(j * batch, batch), pl.ds(row0, rows), :].reshape(batch * rows, hd)
             t1 = (
                 lax.dot_general(q, ck_ref[...], nt, preferred_element_type=jnp.float32) * scale
                 + bias_ref[...]
@@ -165,9 +162,10 @@
                 )
                 * scale
             )
-            row = lax.broadcasted_iota(jnp.int32, (half, half), 0) + row0
-            col = lax.broadcasted_iota(jnp.int32, (half, half), 1) + c * half
-            t2 = jnp.where(row >= col, t2, HIDDEN)
+            row = lax.broadcasted_iota(jnp.int32, (batch, rows, half), 1) + row0
+            col = lax.broadcasted_iota(jnp.int32, (batch, rows, half), 2) + c * half
+            seen = row.reshape(batch * rows, half) >= col.reshape(batch * rows, half)
+            t2 = jnp.where(seen, t2, HIDDEN)
             top = jnp.maximum(
                 jnp.max(t1, axis=1, keepdims=True), jnp.max(t2, axis=1, keepdims=True)
             )
@@ -179,9 +177,14 @@
             ) + jnp.dot(
                 p2.astype(jnp.bfloat16), sv_ref[own_at, :], preferred_element_type=jnp.float32
             )
-            acc_store(pl.multiple_of(j * hd, 128), acc)
-            old = st_ref[st]
-            st_ref[st] = jnp.where(lane == j, top, jnp.where(lane == 64 + j, total, old))
+            stat = st_ref[st]
+            for b in range(batch):
+                at = slice(b * rows, (b + 1) * rows)
+                head = j * batch + b
+                acc_store(pl.multiple_of(head * hd, 128), acc[at])
+                stat = jnp.where(lane == head, top[at], stat)
+                stat = jnp.where(lane == 64 + head, total[at], stat)
+            st_ref[st] = stat
 
         def keep(at, acc):
             acc_own[st, :, pl.ds(at, hd)] = acc
@@ -190,11 +193,16 @@
             acc_send[st, :, pl.ds(at, hd)] = acc.astype(jnp.bfloat16)
 
         def body(j, carry):
-            one(j, theirs, give, st_send, (1 - c) * half)
-            one(j, mine, keep, st_own, c * half)
+            one(j, 1 - c, give, st_send)
+            one(j, c, keep, st_own)
             return carry
 
-        lax.fori_loop(0, per_stage, body, 0)
+        if first == 0:
+            st_own[st] = jnp.zeros((rows, 128), jnp.float32)
+            st_send[st] = jnp.zeros((rows, 128), jnp.float32)
+        lax.fori_loop(first, end, body, 0)
+        if end < blocks:
+            return
         for buf, got, sems in ((acc_send, acc_recv, acc_sems), (st_send, st_recv, st_sems)):
             copy = remote(buf.at[st], got.at[st], sems.at[0, st], sems.at[1, st], core_peer)
             copy.start()
@@ -205,7 +213,7 @@
             remote(buf.at[st], got.at[st], sems.at[0, st], sems.at[1, st], core_peer).wait_recv()
         stat0, stat1 = st_own[st], st_recv[st]
         done = []
-        for j in range(per_stage):
+        for j in range(heads):
             top0, top1 = stat0[:, j : j + 1], stat1[:, j : j + 1]
             top = jnp.maximum(top0, top1)
             f0, f1 = jnp.exp2(top0 - top), jnp.exp2(top1 - top)
@@ -214,8 +222,8 @@
             acc1 = acc_recv[st, :, j * hd : (j + 1) * hd].astype(jnp.float32)
             done.append(((acc0 * (f0 * inv)) + (acc1 * (f1 * inv))).astype(jnp.bfloat16))
         for i in range(group_count):
-            rows = jnp.concatenate(done[i * nsec : (i + 1) * nsec], axis=1)
-            moved = jnp.dot(rows, perm_ref[...], preferred_element_type=jnp.float32).astype(
+            group = jnp.concatenate(done[i * nsec : (i + 1) * nsec], axis=1)
+            moved = jnp.dot(group, perm_ref[...], preferred_element_type=jnp.float32).astype(
                 jnp.bfloat16
             )
             for k in range(nsec):
@@ -250,43 +258,43 @@
         copy.start()
         sends.append(copy)
 
-    for step in range(stages + 3):
-        if step < stages:
-            attend(step)
-        if 1 <= step <= stages:
-            merge(step - 1)
-        if 1 <= step <= stages:
-            w_swap(step - 1).wait_recv()
-            copy = w_pass(step - 1)
-            copy.start()
-            sends.append(copy)
-        if 2 <= step <= stages + 1:
-            forward(step - 2)
-        if 3 <= step:
-            share(step - 3)
-
-    w_own.wait()
-    for i in range(stages):
-        w_pass(i).wait_recv()
-    for st in range(stages):
+    def pass_on(i):
+        w_swap(i).wait_recv()
+        copy = w_pass(i)
+        copy.start()
+        sends.append(copy)
+
+    def ready(st):
         for i, which in enumerate((h, 1 - h)):
             held = a_all.at[st, which, 1 - c]
             remote(held, held, core_send.at[st, i], core_recv.at[st, i], core_peer).wait_recv()
 
+    early, late = blocks // 6, 2 * blocks // 3
+    attend(0, 0, blocks)
+    attend(1, 0, early)
+    merge(0)
+    pass_on(0)
+    attend(1, early, late)
+    pass_on(1)
+    forward(0)
+    attend(1, late, blocks)
+    pass_on(2)
+    merge(1)
+    share(0)
+    w_own.wait()
+    for i in range(parts):
+        w_pass(i).wait_recv()
+    ready(0)
+
     chunk = right_send.shape[2]
     chunks = ncols // chunk
 
-    def product(which, n):
+    def product(st, which, n):
         at = pl.ds(pl.multiple_of(n * chunk, 128), chunk)
-        total = jnp.zeros((slice_len, chunk), jnp.float32)
+        total = jnp.zeros((tokens, chunk), jnp.float32)
         for hh in range(2):
-            for st in range(stages):
-                left = a_all[st, hh, :, which].reshape(slice_len, kcols)
-                total += jnp.dot(
-                    left,
-                    w_all[hh, st * kcols : (st + 1) * kcols, at],
-                    preferred_element_type=jnp.float32,
-                )
+            left = a_all[st, hh, :, which].reshape(tokens, depth)
+            total += jnp.dot(left, w_all[hh, :, at], preferred_element_type=jnp.float32)
         return total
 
     last = nsec - 1
@@ -300,14 +308,19 @@
         to = (g, jnp.clip(s + step, 0, last), c, h)
         return remote(out.at[m], got.at[m], ssem.at[m], rsem.at[m], to)
 
+    per_stage = last * chunks
+
+    def valid(m, behind):
+        return (m >= 0) & (m < stages * per_stage) & ((m // chunks) % last < last - behind)
+
     def wave(t, carry):
         for way in ways:
             out, got, _, _, behind, _, owner = way
             m = t - behind
 
-            @pl.when((m >= 0) & (m < chunks * (last - behind)))
+            @pl.when(valid(m, behind))
             def _():
-                total = product(owner(m // chunks), m % chunks)
+                total = product(m // per_stage, owner((m // chunks) % last), m % chunks)
 
                 @pl.when(behind == 0)
                 def _():
@@ -318,7 +331,7 @@
                     hop(way, m).wait_recv()
                     out[m] = (total + got[m].astype(jnp.float32)).astype(jnp.bfloat16)
 
-                @pl.when(m >= 2)
+                @pl.when(valid(m - 2, behind))
                 def _():
                     hop(way, m - 2).wait_send()
 
@@ -326,28 +339,41 @@
 
         return carry
 
-    lax.fori_loop(0, chunks * last + last, wave, 0)
-
-    for n in range(chunks):
-        kept[...] = product(s, n)
+    lax.fori_loop(0, per_stage // 3, wave, 0)
+    forward(1)
+    lax.fori_loop(per_stage // 3, 2 * per_stage // 3, wave, 0)
+    share(1)
+    lax.fori_loop(2 * per_stage // 3, per_stage, wave, 0)
+    ready(1)
+    lax.fori_loop(per_stage, stages * per_stage + last, wave, 0)
+
+    for st in range(stages):
+        for n in range(chunks):
+            kept[...] = product(st, s, n)
+            for way in ways:
+                got, behind = way[1], way[4]
+                m = st * per_stage + (last - behind) * chunks + n
+
+                @pl.when(behind > 0)
+                def _():
+                    hop(way, m).wait_recv()
+                    kept[...] += got[m].astype(jnp.float32)
+
+            out_ref[st * tokens : (st + 1) * tokens, n * chunk : (n + 1) * chunk] = kept[
+                ...
+            ].astype(jnp.bfloat16)
+
+    def drain(m, carry):
         for way in ways:
-            got, behind = way[1], way[4]
-            m = (last - behind) * chunks + n
-
-            @pl.when(behind > 0)
+            behind = way[4]
+
+            @pl.when(valid(m, behind) & jnp.logical_not(valid(m + 2, behind)))
             def _():
-                hop(way, m).wait_recv()
-                kept[...] += got[m].astype(jnp.float32)
-
-        out_ref[:, n * chunk : (n + 1) * chunk] = kept[...].astype(jnp.bfloat16)
-    for way in ways:
-        count = chunks * (last - way[4])
-        for back in (2, 1):
-
-            @pl.when(count >= back)
-            def _():
-                hop(way, count - back).wait_send()
-
+                hop(way, m).wait_send()
+
+        return carry
+
+    lax.fori_loop(0, stages * per_stage, drain, 0)
     for copy in sends:
         copy.wait_send()
 
@@ -355,15 +381,14 @@
 def fused(queries, slice_kv, cache_keys, cache_values, block_table, slice_index, out_weight):
     slice_len, heads, hd = queries.shape
     nsec = lax.axis_size("section")
-    stages = 3
+    stages = 2
     half = slice_len // 2
-    per_stage = heads // stages
-    width = per_stage * hd
-    kcols = per_stage // nsec * hd
+    rows = half // stages
+    width = heads * hd
     ncols = out_weight.shape[2] // 2
     depth = out_weight.shape[0] * out_weight.shape[1]
-    chunk = 512 if ncols % 512 == 0 else 128
-    items = (nsec - 1) * (ncols // chunk)
+    chunk = ncols // 2
+    items = stages * (nsec - 1) * (ncols // chunk)
     live = live_keys(block_table, slice_index, cache_keys.shape[2], cache_keys.shape[1])
     bias = jnp.where(live, 0.0, HIDDEN).astype(jnp.float32)[None, :]
     piece = hd // nsec
@@ -383,18 +408,18 @@
         out_specs=vmem,
         scratch_shapes=[
             pltpu.VMEM((2, depth, ncols), bf16),
-            pltpu.VMEM((stages, 2, 2, nsec, half, kcols), bf16),
-            pltpu.VMEM((stages, nsec, half, kcols), bf16),
-            pltpu.VMEM((stages, half, width), f32),
-            pltpu.VMEM((stages, half, width), bf16),
-            pltpu.VMEM((stages, half, width), bf16),
-            pltpu.VMEM((stages, half, 128), f32),
-            pltpu.VMEM((stages, half, 128), f32),
-            pltpu.VMEM((stages, half, 128), f32),
-            *[pltpu.VMEM((items, slice_len, chunk), bf16)] * 4,
-            pltpu.VMEM((slice_len, chunk), f32),
+            pltpu.VMEM((stages, 2, 2, nsec, rows, depth), bf16),
+            pltpu.VMEM((stages, nsec, rows, depth), bf16),
+            pltpu.VMEM((stages, rows, width), f32),
+            pltpu.VMEM((stages, rows, width), bf16),
+            pltpu.VMEM((stages, rows, width), bf16),
+            pltpu.VMEM((stages, rows, 128), f32),
+            pltpu.VMEM((stages, rows, 128), f32),
+            pltpu.VMEM((stages, rows, 128), f32),
+            *[pltpu.VMEM((items, 2 * rows, chunk), bf16)] * 4,
+            pltpu.VMEM((2 * rows, chunk), f32),
             dma,
-            dma((4, stages)),
+            dma((4, 3)),
             dma((2, stages)),
             dma((2, stages)),
             dma((stages, nsec - 1)),
@@ -408,7 +433,7 @@
             collective_id=0, has_side_effects=True, vmem_limit_bytes=52 * 1024 * 1024
         ),
     )(
-        queries.reshape(slice_len, heads * hd),
+        jnp.swapaxes(queries, 0, 1),
         cache_keys.reshape(-1, hd),
         cache_values.reshape(-1, hd),
         slice_kv[:, 0],
@@ -429,9 +454,10 @@
         and arrays[6].shape[0] * arrays[6].shape[1] % 96 == 0
         and hd == 128
         and slice_len % 256 == 0
-        and heads % (3 * nsec) == 0
-        and heads // 3 <= 64
-        and arrays[6].shape[2] % 256 == 0
+        and heads % nsec == 0
+        and heads % 4 == 0
+        and heads <= 64
+        and arrays[6].shape[2] % 512 == 0
     )
     return fused(*arrays) if fits else plain(*arrays)
 

time: 113 us -> 104 us (0.920)
  Pallas kernels: 103 us -> 95.1 us
    pallas_call x1, Pallas kernels: 103 us -> 95.1 us  [fused(): pl.pallas_call(functools.partial(kernel, (slice_len, heads, hd, nsec, sta...]
where the time goes in v3:
time: 104 us; the launch traced here: 103 us
  Pallas kernels  95.1 us (91%)
  local copies, waits for them, and re-layouts  6.47 us (6%)
    pallas_call x1, Pallas kernels, fused(): pl.pallas_call(functools.partial(kernel, (slice_len, heads, hd, nsec, sta...  95.1 us
    unnamed x10, local copies, waits for them, and re-layouts  3.91 us

profile of v3, /device:TPU:9, one launch (start us, length us, event | category | flops | bytes accessed | tf_op | source)
XLA Modules:
  0.0 102.5 jit_solution(9093866761741724618)
XLA Ops:
  0.0 0.0 copy-start
  0.0 1.2 %dynamic_slice.10 = s32[1]{0:T(128)} dynamic-slice(s32[4]{0:T(128)} %param.13, s32[]{:T(128)S(6)} %select_n.26), dynamic_slice_sizes={1} | dynamic-slice | bytes 12 | tf_op jit(solution)/shard_map/dynamic_slice | solution.py:25
  1.9 0.0 copy-done
  1.9 0.1 select_reduce_fusion
  2.1 0.1 dynamic-slice_select_fusion
  2.1 0.1 broadcast_in_dim.30
  2.2 1.2 %fusion = (bf16[256,1,128]{2,1,0:T(2,128)(2,1)S(1)}, bf16[256,1,128]{2,1,0:T(2,128)(2,1)S(1)}) fusion(bf16[256,2,128]{2,1,0:T(2,128)(2,1)} %param.9), kind=kLoop, calls=%fused_computation.8 | loop fusion | bytes 262144 | tf_op jit(solution)/shard_map/slice | solution.py:440
  3.5 0.0 copy-start.1
  3.5 0.0 copy-start.2
  3.5 0.0 copy-start.3
  3.5 3.0 %copy.20 = bf16[256,24,128]{2,0,1:T(8,128)(2,1)} copy(bf16[256,24,128]{2,1,0:T(8,128)(2,1)} %param.8) | data formatting | bytes 3145728 | tf_op args[0]
  6.5 0.0 copy-done.1
  6.5 0.0 copy-done.2
  6.5 0.0 copy-done.3
  6.5 95.1 %shard_map.82 = bf16[256,1536]{1,0:T(8,128)(2,1)S(1)} custom-call(bf16[24,256,128]{2,1,0:T(8,128)(2,1)} %bitcast.17, bf16[1024,128]{1,0:T(8,128)(2,1)S(1)} %bitcast.14, bf16[1024,128]{1,0:T(8,128)(2,1)S(1)} %bitcast.15, bf16[256,128]{1,0:T(8,128)(2,1)S(1)} %get-tuple-element.8.sk_ref, bf16[256,128]{1,0:T(8,128)(2,1)S(1)} %get-tuple-element.7.sv_ref, ...), custom_call_target="tpu_custom_call" | custom-call | tf_op jit(solution)/shard_map/pallas_call | solution.py:404
  101.6 0.9 copy.22
  (3 shorter events, 0.0 us)
Async XLA Ops:
  0.0 1.9 %copy-start = (s32[4,16]{1,0:T(4,128)S(1)}, s32[4,16]{1,0:T(4,128)}, u32[]{:S(2)}) copy-start(s32[4,16]{1,0:T(4,128)} %param.12) | copy-start | bytes 772
  3.5 3.0 %copy-start.1 = (bf16[512,512]{1,0:T(8,128)(2,1)S(1)}, bf16[512,512]{1,0:T(8,128)(2,1)}, u32[]{:S(2)}) copy-start(bf16[512,512]{1,0:T(8,128)(2,1)} %constant.28.clone.perm_ref) | copy-start | bytes 1572868
  3.5 3.0 %copy-start.2 = (bf16[1,8,128,128]{3,2,1,0:T(8,128)(2,1)S(1)}, bf16[1,8,128,128]{3,2,1,0:T(8,128)(2,1)}, u32[]{:S(2)}) copy-start(bf16[1,8,128,128]{3,2,1,0:T(8,128)(2,1)} %param.10) | copy-start | bytes 786436
  3.5 3.0 %copy-start.3 = (bf16[1,8,128,128]{3,2,1,0:T(8,128)(2,1)S(1)}, bf16[1,8,128,128]{3,2,1,0:T(8,128)(2,1)}, u32[]{:S(2)}) copy-start(bf16[1,8,128,128]{3,2,1,0:T(8,128)(2,1)} %param.11) | copy-start | bytes 786436
